TPU v7x, 256 devices: a whole 4x4x8 slice. The times are simulated.
256 devices in a mesh: ctx: 32 (over z, x), head: 8 (over y, core).
Axes of the slice: x: 4, y: 4, z: 8, core: 2. Of those that a mesh axis runs over, the one named last changes fastest.
Arguments:
- queries: bfloat16 [16384, 2048], P('ctx', 'head'), may hold values from -6 to 6
- keys: bfloat16 [16384, 2048], P('ctx', 'head'), may hold values from -6 to 6
- values: bfloat16 [16384, 2048], P('ctx', 'head'), may hold values from -6 to 6
- frame_ids: int32 [64], replicated, may hold values from 0 to 31, never falling along the last dimension, each value on 1 to 4 neighbouring positions
- half_order: int32 [64], replicated, may hold values from 0 to 63, as said below
- out_weight: bfloat16 [2048, 4096], P('head'), may hold values from -0.125 to 0.125
Outputs:
- mixed: bfloat16 [16384, 4096], P('ctx', 'head')
Inputs may be any that keep to these rules, and one draw needn't show every extreme that they name: `frame_ids`: never falling along the sequence; every frame number is used, by 1 to 4 blocks, and some frame by exactly 4. `half_order`: each half number appears once; device c of ctx stores halves 2 * c and 2 * c + 1; half 2 * c holds a sequence half below 32 and half 2 * c + 1 holds its mirror, 63 minus it.
All inputs are finite; a program needn't handle non-finite values.
Results may differ from a plain program's by a relative error of at most 0.02.
Values may be sent and summed in bfloat16 or wider, within the bound.
A program may use at most 128 MiB of HBM per device.

v0:
```python
import math

import jax
import jax.numpy as jnp
from jax import lax
from jax.sharding import PartitionSpec as P

HD = 128
BLOCK = 256


def per_device(queries, keys, values, frame_ids, half_order, out_weight):
    rows_dev = queries.shape[0]
    heads_dev = queries.shape[1] // HD
    half_rows = rows_dev // 2
    per_half = half_rows // BLOCK
    block_count = frame_ids.shape[0]
    half_count = half_order.shape[0]
    slot_ids = jnp.arange(block_count, dtype=jnp.int32)
    pick_half = (slot_ids // per_half)[:, None] == jnp.arange(half_count, dtype=jnp.int32)[None, :]
    seq_half = jnp.sum(jnp.where(pick_half, half_order[None, :], 0), axis=1)
    seq_block = seq_half * per_half + slot_ids % per_half
    slot_frame = jnp.sum(
        jnp.where(seq_block[:, None] == slot_ids[None, :], frame_ids[None, :], 0), axis=1
    )

    def frames_of(first_row, row_count):
        stored = (first_row + jnp.arange(row_count, dtype=jnp.int32)) // BLOCK
        return jnp.sum(
            jnp.where(stored[:, None] == slot_ids[None, :], slot_frame[None, :], 0), axis=1
        )

    query_frame = frames_of(lax.axis_index("ctx") * rows_dev, rows_dev)
    score_scale = 1.0 / math.sqrt(HD)
    queries3 = queries.reshape(rows_dev, heads_dev, HD)
    initial = (
        jnp.full((heads_dev, rows_dev), -1e30, jnp.float32),
        jnp.zeros((heads_dev, rows_dev), jnp.float32),
        jnp.zeros((heads_dev, rows_dev, HD), jnp.float32),
    )
    carried = initial
    key_rows = lax.all_gather(keys, "ctx", axis=0, tiled=True)
    value_rows = lax.all_gather(values, "ctx", axis=0, tiled=True)
    key_count = key_rows.shape[0]
    tile_rows = math.gcd(key_count, 512)
    tile_count = key_count // tile_rows
    key_tiles = key_rows.reshape(tile_count, tile_rows, heads_dev, HD)
    value_tiles = value_rows.reshape(tile_count, tile_rows, heads_dev, HD)

    def one_tile(status, inputs):
        key_tile, value_tile, number = inputs
        allowed = frames_of(number * tile_rows, tile_rows)[None, :] <= query_frame[:, None]
        running, totals, accumulated = status
        scores = (
            jnp.einsum("qhd,khd->hqk", queries3, key_tile, preferred_element_type=jnp.float32)
            * score_scale
        )
        scores = jnp.where(allowed[None], scores, -1e30)
        newmax = jnp.maximum(running, jnp.max(scores, axis=2))
        weights = jnp.exp(scores - newmax[..., None])
        shrink = jnp.exp(running - newmax)
        totals = totals * shrink + jnp.sum(weights, axis=2)
        product = jnp.einsum(
            "hqk,khd->hqd",
            weights.astype(jnp.bfloat16),
            value_tile,
            preferred_element_type=jnp.float32,
        )
        accumulated = accumulated * shrink[..., None] + product
        status = (newmax, totals, accumulated)
        return (status, None)

    carried, _ = lax.scan(
        one_tile, carried, (key_tiles, value_tiles, jnp.arange(tile_count, dtype=jnp.int32))
    )
    running, totals, accumulated = carried
    attended = (accumulated / totals[..., None]).astype(jnp.bfloat16)
    attended = attended.transpose(1, 0, 2).reshape(rows_dev, heads_dev * HD)
    partial_value = jnp.dot(attended, out_weight, preferred_element_type=jnp.float32)
    mixed = lax.psum_scatter(
        partial_value.astype(jnp.bfloat16), "head", scatter_dimension=1, tiled=True
    )
    return mixed


def solution(mesh):
    placed = (P("ctx", "head"), P("ctx", "head"), P("ctx", "head"), P(), P(), P("head", None))
    return jax.shard_map(
        per_device, mesh=mesh, in_specs=placed, out_specs=P("ctx", "head"), check_vma=False
    )
```

profile of v0, /device:TPU:1, one launch (start us, length us, event | category | flops | bytes accessed | tf_op | source)
XLA Modules:
  0.0 413.8 jit_solution(14227581617582951357)
XLA Ops:
  11.1 100.6 %all-gather.3.cloned.1.call-done = bf16[16384,256]{1,0:T(8,128)(2,1)} async-done(((bf16[512,256]{1,0:T(8,128)(2,1)}), bf16[16384,256]{1,0:T(8,128)(2,1)}) %all-gather.3.cloned.1.call-update) | async-done | bytes 8388624 | tf_op jit(solution)/shard_map/all_gather | solution.py:42
  111.7 12.5 %reshape.94 = bf16[32,512,2,128]{3,2,1,0:T(2,128)(2,1)} reshape(bf16[16384,256]{1,0:T(8,128)(2,1)} %all-gather.3.cloned.1.call-done) | data formatting | bytes 16777216 | tf_op jit(solution)/shard_map/reshape | solution.py:47
  124.2 85.5 %all-gather.5.cloned.1.call-done = bf16[16384,256]{1,0:T(8,128)(2,1)} async-done(((bf16[512,256]{1,0:T(8,128)(2,1)}), bf16[16384,256]{1,0:T(8,128)(2,1)}) %all-gather.5.cloned.1.call-update) | async-done | bytes 8388624 | tf_op jit(solution)/shard_map/all_gather | solution.py:43
  209.7 12.5 %reshape.95 = bf16[32,512,2,128]{3,2,1,0:T(2,128)(2,1)} reshape(bf16[16384,256]{1,0:T(8,128)(2,1)} %all-gather.5.cloned.1.call-done) | data formatting | bytes 16777216 | tf_op jit(solution)/shard_map/reshape | solution.py:48
  222.3 146.2 %while.17 = (s32[]{:T(128)}, f32[2,512]{1,0:T(2,128)S(1)}, f32[2,512]{1,0:T(2,128)S(1)}, f32[2,512,128]{2,1,0:T(8,128)S(1)}, s32[32]{0:T(128)S(1)}, /*index=5*/s...) while((s32[]{:T(128)}, f32[2,512]{1,0:T(2,128)S(1)}, ...), condition=%wide.region_7.8_spmd.clone, body=%wide.region_3.7_spmd.clone.sunk | while | flops 272871936 | bytes 9775537 | solution.py:73
  223.7 1.4 constant_dynamic-slice_fusion.3
  228.3 1.4 constant_dynamic-slice_fusion.3
  232.9 1.4 constant_dynamic-slice_fusion.3
  237.4 1.4 constant_dynamic-slice_fusion.3
  242.0 1.4 constant_dynamic-slice_fusion.3
  246.6 1.4 constant_dynamic-slice_fusion.3
  251.1 1.4 constant_dynamic-slice_fusion.3
  260.3 1.4 constant_dynamic-slice_fusion.3
  269.4 1.4 constant_dynamic-slice_fusion.3
  278.6 1.4 constant_dynamic-slice_fusion.3
  287.7 1.4 constant_dynamic-slice_fusion.3
  301.4 1.4 constant_dynamic-slice_fusion.3
  310.5 1.4 constant_dynamic-slice_fusion.3
  319.7 1.4 constant_dynamic-slice_fusion.3
  328.8 1.4 constant_dynamic-slice_fusion.3
  351.7 1.4 constant_dynamic-slice_fusion.3
  360.8 1.4 constant_dynamic-slice_fusion.3
  368.7 3.2 convolution_convert_fusion
  371.9 35.4 %reduce-scatter.2.cloned.1.call-done = bf16[512,512]{1,0:T(8,128)(2,1)} async-done(((bf16[512,4096]{1,0:T(8,128)(2,1)}), bf16[512,512]{1,0:T(8,128)(2,1)}) %reduce-scatter.2.cloned.1.call-update) | async-done | bytes 524304 | tf_op jit(solution)/shard_map/reduce_scatter | solution.py:80
  (355 shorter events, 107.0 us)
Async XLA Ops:
  6.5 362.2 %copy-start = (bf16[256,4096]{1,0:T(8,128)(2,1)S(1)}, bf16[256,4096]{1,0:T(8,128)(2,1)}, u32[]{:S(2)}) copy-start(bf16[256,4096]{1,0:T(8,128)(2,1)} %param.13) | copy-start | bytes 6291460
  6.5 105.1 %all-gather.3.cloned.1.call-start = ((), (), s32[]{:S(2)}) async-start(), calls=%async_computation.1 | async-start | bytes 8650752 | tf_op jit(solution)/shard_map/all_gather | solution.py:42
  7.3 202.5 %all-gather.5.cloned.1.call-start = ((), (), s32[]{:S(2)}) async-start(), calls=%async_computation.2 | async-start | bytes 8650752 | tf_op jit(solution)/shard_map/all_gather | solution.py:43
  8.0 399.3 %reduce-scatter.2.cloned.1.call-start = ((), (), s32[]{:S(2)}) async-start(), calls=%async_computation.3 | async-start | bytes 4718592 | tf_op jit(solution)/shard_map/reduce_scatter | solution.py:80
Sparse Core Ops, SparseCore 0:
  9.9 101.6 all-gather.2
  114.3 95.4 all-gather.4
  372.1 35.1 reduce-scatter.1
where the time goes:
time: 417 us; the launch traced here: 414 us
  waiting for transfers between devices  223 us (53%)
  local copies, waits for them, and re-layouts  90 us (22%)
  matrix products  45 us (11%)
  other arithmetic  22.6 us (5%)
  loops' own time  20.2 us (5%)
  between operations  13.2 us (3%)
    all_gather x1, waiting for transfers between devices, per_device(): key_rows = lax.all_gather(keys, 'ctx', axis=0, tiled=True)  101 us
    all_gather x1, waiting for transfers between devices, per_device(): value_rows = lax.all_gather(values, 'ctx', axis=0, tiled=True)  85.5 us
    dynamic_slice x64, local copies, waits for them, and re-layouts, per_device(): lax.scan(one_tile, carried, (key_tiles, value_tiles, jnp.arange(tile_coun...  63.3 us
    reduce_scatter x1, waiting for transfers between devices, per_device(): lax.psum_scatter(partial_value.astype(jnp.bfloat16), 'head', scatter_dime...  35.4 us
    dot_general x32, matrix products, one_tile(): jnp.einsum('hqk,khd->hqd', weights.astype(jnp.bfloat16), value_tile, pref...  23.6 us
    another operation x1, loops' own time, per_device(): lax.scan(one_tile, carried, (key_tiles, value_tiles, jnp.arange(tile_coun...  20.2 us
    dot_general x32, matrix products, one_tile(): jnp.einsum('qhd,khd->hqk', queries3, key_tile, preferred_element_type=jnp...  18.2 us
    reshape x1, local copies, waits for them, and re-layouts, per_device(): key_tiles = key_rows.reshape(tile_count, tile_rows, heads_dev, HD)  12.5 us
  transfers between devices with their start and end apart: 3, of which 3 were waited for; matrix products, arithmetic and copies ran while one was open for 4% of the time, Pallas kernels for 0%

commit v1 on v0

v1 whole, which is shorter than its diff:
```python
import functools
import math

import jax
import jax.numpy as jnp
from jax import lax
from jax.experimental import pallas as pl
from jax.experimental.pallas import tpu as pltpu
from jax.sharding import PartitionSpec as P

HD = 128
HALF = 256
ROWS = 512
NX, NY, NZ = 4, 4, 8
COLS = 512
SCALE = math.log2(math.e) / math.sqrt(HD)
HIDE = 2e30
LOWEST = -1e30
NT = (((1,), (1,)), ((), ()))
NN = (((1,), (0,)), ((), ()))


def kernel(
    order_ref, frames_ref, q_hbm, k_hbm, v_hbm, w_hbm, out_ref,
    q_buf, kv, acc, top, total, att, att_out, w_buf, out_acc,
    q_recv, kv_recv, att_recv, w_recv,
    first_send, ring_send, side_send, w_send, out_send, att_send, att_side_send,
):
    ctx, j = lax.axis_index("ctx"), lax.axis_index("head")
    z, x = ctx // NX, ctx % NX
    y, b = j // 2, j % 2
    slot, owner = x % 2, x // 2
    side = {"ctx": ctx, "head": y * 2 + 1 - b}
    up = {"ctx": ((z + 1) % NZ) * NX + x, "head": j}
    down = {"ctx": ((z + NZ - 1) % NZ) * NX + x, "head": j}
    y_up = {"ctx": ctx, "head": ((y + 1) % NY) * 2 + b}
    y_down = {"ctx": ctx, "head": ((y + NY - 1) % NY) * 2 + b}

    def across(i):
        return {"ctx": z * NX + 2 * b + i, "head": y * 2 + owner}

    def is_self(i):
        return jnp.logical_and(2 * b + i == x, owner == b)

    def remote(src, dst, send, recv, device):
        return pltpu.make_async_remote_copy(
            src_ref=src, dst_ref=dst, send_sem=send, recv_sem=recv,
            device_id=device, device_id_type=pl.DeviceIdType.MESH,
        )

    def arrived(ref, sem):
        pltpu.make_async_copy(ref, ref, sem).wait()

    def send_or_keep(i, src, dst, send, recv):
        @pl.when(is_self(i))
        def _():
            pltpu.make_async_copy(src, dst, recv).start()

        @pl.when(jnp.logical_not(is_self(i)))
        def _():
            remote(src, dst, send, recv, across(i)).start()

    def sent_across(i, src, dst, send, recv):
        @pl.when(jnp.logical_not(is_self(i)))
        def _():
            remote(src, dst, send, recv, across(i)).wait_send()

    barrier = pltpu.get_barrier_semaphore()
    for device in [{"ctx": ctx, "head": (j + d) % (2 * NY)} for d in range(1, 2 * NY)] + [up, down]:
        pl.semaphore_signal(barrier, inc=1, device_id=device, device_id_type=pl.DeviceIdType.MESH)
    for i in range(2):
        @pl.when(jnp.logical_not(is_self(i)))
        def _():
            pl.semaphore_signal(barrier, inc=1, device_id=across(i), device_id_type=pl.DeviceIdType.MESH)
    pl.semaphore_wait(barrier, 2 * NY - 1 + 2 + 2 - jnp.where(owner == b, 1, 0))

    def first_copies(i):
        cols = pl.ds(i * HD, HD)
        return (
            (k_hbm.at[:, cols], kv.at[slot, 0], first_send.at[i, 0], kv_recv.at[slot]),
            (v_hbm.at[:, cols], kv.at[slot, 1], first_send.at[i, 1], kv_recv.at[slot]),
            (q_hbm.at[:, cols], q_buf.at[slot], first_send.at[i, 2], q_recv.at[slot]),
        )

    for what in range(3):
        for i in range(2):
            send_or_keep(i, *first_copies(i)[what])

    def w_copy(n):
        ry, other = n % NY, n // NY
        target = ((y + ry) % NY) * 2 + (1 - b if other else b)
        place = (NY - ry) % NY + NY * other
        src = w_hbm.at[:, pl.ds(pl.multiple_of(target * COLS, COLS), COLS)]
        if n == 0:
            return pltpu.make_async_copy(src, w_buf.at[0], w_recv.at[0])
        return remote(src, w_buf.at[place], w_send.at[n], w_recv.at[place], {"ctx": ctx, "head": target})

    for n in range(2 * NY):
        w_copy(n).start()

    acc[...] = jnp.zeros_like(acc)
    total[...] = jnp.zeros_like(total)
    top[...] = jnp.full_like(top, LOWEST)

    def frame(c, h):
        return frames_ref[order_ref[2 * c + h]]

    q_frames = [frame(z * NX + 2 * b + n // 2, n % 2) for n in range(4)]

    def shards(g, core):
        s = 1 + (g - 1) // 2
        r = jnp.where(g == 0, 0, s)
        rc = (g + 1) % 2
        ends = jnp.logical_or(g == 0, g == 7)
        rc_a = jnp.where(ends, 0, rc)
        rc_b = jnp.where(ends, 1, rc)
        return (
            ((z + NZ - r) % NZ) * NX + 2 * core + rc_a,
            ((z + r) % NZ) * NX + 2 * core + rc_b,
        )

    def attend(first, g, core):
        c_a, c_b = shards(g, core)
        k_frames = [frame(c, h) for c in (c_a, c_b) for h in range(2)]
        keys = jnp.concatenate([kv[first, 0], kv[first + 1, 0]], axis=0)
        values = jnp.concatenate([kv[first, 1], kv[first + 1, 1]], axis=0)
        values = jnp.concatenate([values, jnp.ones_like(values)], axis=1)
        for t in range(4):
            rows = pl.ds(t * HALF, HALF)
            queries = q_buf[t // 2, pl.ds((t % 2) * HALF, HALF), :]
            scores = lax.dot_general(queries, keys, NT, preferred_element_type=jnp.float32)
            hide = [jnp.where(f <= q_frames[t], 0.0, HIDE) for f in k_frames]
            best = None
            for h in range(4):
                part = jnp.maximum(
                    scores[:, h * HALF : h * HALF + HD], scores[:, h * HALF + HD : (h + 1) * HALF]
                ) - hide[h]
                best = part if best is None else jnp.maximum(best, part)
            old = top[rows, :]
            new = jnp.maximum(old, jnp.max(best, axis=1, keepdims=True) * SCALE)
            weights = []
            for h in range(4):
                base = new + hide[h]
                for n in range(2):
                    col = h * HALF + n * HD
                    weights.append(jnp.exp2(scores[:, col : col + HD] * SCALE - base).astype(jnp.bfloat16))
            weights = jnp.concatenate(weights, axis=1)
            product = lax.dot_general(weights, values, NN, preferred_element_type=jnp.float32)
            shrink = jnp.exp2(old - new)
            acc[rows, :] = acc[rows, :] * shrink + product[:, :HD]
            total[rows, :] = total[rows, :] * shrink + product[:, HD:]
            top[rows, :] = new

    def ring_copy(e, later, sem, device):
        return remote(kv.at[e], kv.at[later], ring_send.at[sem], kv_recv.at[later], device)

    def side_copy(e):
        return remote(kv.at[e], kv.at[16 + e], side_send.at[e], kv_recv.at[16 + e], side)

    def first_ring(e, act):
        act(ring_copy(e, 2 + 2 * e, e, up))
        act(ring_copy(e, 3 + 2 * e, 16 + e, down))

    start = lambda copy: copy.start()
    sent = lambda copy: copy.wait_send()

    def step(g, carry):
        @pl.when(g == 0)
        def _():
            for e in range(2):
                arrived(kv.at[e], kv_recv.at[e])
                first_ring(e, start)
                side_copy(e).start()
            for n in range(2):
                arrived(q_buf.at[n], q_recv.at[n])

        @pl.when(jnp.logical_and(g >= 1, g <= 7))
        def _():
            a, c = 2 * g, 2 * g + 1
            arrived(kv.at[a], kv_recv.at[a])
            @pl.when(g <= 4)
            def _():
                ring_copy(a, a + 4, a, up).start()
            @pl.when(g == 5)
            def _():
                ring_copy(10, 14, 10, up).start()
            arrived(kv.at[c], kv_recv.at[c])
            @pl.when(g <= 4)
            def _():
                ring_copy(c, c + 4, c, down).start()
            @pl.when(g == 6)
            def _():
                ring_copy(13, 15, 13, down).start()
            side_copy(a).start()
            side_copy(c).start()

        @pl.when(g <= 7)
        def _():
            attend(2 * g, g, b)

        @pl.when(g >= 1)
        def _():
            n = 16 + 2 * (g - 1)
            arrived(kv.at[n], kv_recv.at[n])
            arrived(kv.at[n + 1], kv_recv.at[n + 1])
            attend(n, g - 1, 1 - b)

        return carry

    lax.fori_loop(0, 9, step, 0)

    def out_copy(i):
        return (att_out.at[i], att.at[0, 0, slot], out_send.at[i], att_recv.at[0, 0, slot])

    for i in range(2):
        rows = pl.ds(i * ROWS, ROWS)
        att_out[i] = (acc[rows, :] / total[rows, :]).astype(jnp.bfloat16)
        send_or_keep(i, *out_copy(i))

    def y_copy(ry, later, n, sem, device):
        return remote(att.at[0, ry, n], att.at[0, later, n], att_send.at[sem], att_recv.at[0, later, n], device)

    def att_side(ry, n):
        return remote(
            att.at[0, ry, n], att.at[1, ry, n], att_side_send.at[ry, n], att_recv.at[1, ry, n], side
        )

    y_copies = [
        y_copy(0, 3, 0, 0, y_up), y_copy(0, 1, 0, 1, y_down),
        y_copy(0, 3, 1, 2, y_up), y_copy(0, 1, 1, 3, y_down),
        y_copy(3, 2, 0, 4, y_up), y_copy(1, 2, 1, 5, y_down),
    ]

    def project(core, ry, first=False):
        place = ry + NY * core
        arrived(w_buf.at[place], w_recv.at[place])
        rows = jnp.concatenate([att[core, ry, 0], att[core, ry, 1]], axis=1)
        product = lax.dot_general(rows, w_buf[place], NN, preferred_element_type=jnp.float32)
        out_acc[...] = product if first else out_acc[...] + product

    for n in range(2):
        arrived(att.at[0, 0, n], att_recv.at[0, 0, n])
        y_copies[2 * n].start()
        y_copies[2 * n + 1].start()
        att_side(0, n).start()
    project(0, 0, True)
    for n in range(2):
        arrived(att.at[1, 0, n], att_recv.at[1, 0, n])
    project(1, 0)
    arrived(att.at[0, 3, 0], att_recv.at[0, 3, 0])
    y_copies[4].start()
    att_side(3, 0).start()
    arrived(att.at[0, 1, 0], att_recv.at[0, 1, 0])
    att_side(1, 0).start()
    arrived(att.at[0, 1, 1], att_recv.at[0, 1, 1])
    y_copies[5].start()
    att_side(1, 1).start()
    arrived(att.at[0, 3, 1], att_recv.at[0, 3, 1])
    att_side(3, 1).start()
    project(0, 3)
    project(0, 1)
    for ry in (3, 1):
        for n in range(2):
            arrived(att.at[1, ry, n], att_recv.at[1, ry, n])
        project(1, ry)
    for n in range(2):
        arrived(att.at[0, 2, n], att_recv.at[0, 2, n])
        att_side(2, n).start()
    project(0, 2)
    for n in range(2):
        arrived(att.at[1, 2, n], att_recv.at[1, 2, n])
    project(1, 2)
    out_ref[...] = out_acc[...].astype(out_ref.dtype)

    for i in range(2):
        for what in range(3):
            sent_across(i, *first_copies(i)[what])
        sent_across(i, *out_copy(i))
    for n in range(1, 2 * NY):
        w_copy(n).wait_send()
    for e in range(2):
        first_ring(e, sent)
    for e in range(2, 10):
        ring_copy(e, e + 4, e, up).wait_send()
    ring_copy(10, 14, 10, up).wait_send()
    ring_copy(13, 15, 13, down).wait_send()
    for e in range(16):
        side_copy(e).wait_send()
    for copy in y_copies:
        copy.wait_send()
    for ry in range(NY):
        for n in range(2):
            att_side(ry, n).wait_send()


def per_device(queries, keys, values, frame_ids, half_order, out_weight):
    any_space = pl.BlockSpec(memory_space=pl.ANY)
    smem = pl.BlockSpec(memory_space=pltpu.SMEM)
    bf16, f32 = jnp.bfloat16, jnp.float32
    dma = pltpu.SemaphoreType.DMA
    return pl.pallas_call(
        kernel,
        out_shape=jax.ShapeDtypeStruct((ROWS, COLS), bf16),
        in_specs=[smem, smem, any_space, any_space, any_space, any_space],
        out_specs=pl.BlockSpec(memory_space=pltpu.VMEM),
        scratch_shapes=[
            pltpu.VMEM((2, ROWS, HD), bf16),
            pltpu.VMEM((32, 2, ROWS, HD), bf16),
            pltpu.VMEM((2 * ROWS, HD), f32),
            pltpu.VMEM((2 * ROWS, HD), f32),
            pltpu.VMEM((2 * ROWS, HD), f32),
            pltpu.VMEM((2, NY, 2, ROWS, HD), bf16),
            pltpu.VMEM((2, ROWS, HD), bf16),
            pltpu.VMEM((2 * NY, 2 * HD, COLS), bf16),
            pltpu.VMEM((ROWS, COLS), f32),
            dma((2,)), dma((32,)), dma((2, NY, 2)), dma((2 * NY,)),
            dma((2, 3)), dma((18,)), dma((16,)), dma((2 * NY,)), dma((2,)), dma((6,)), dma((NY, 2)),
        ],
        compiler_params=pltpu.CompilerParams(
            collective_id=0, has_side_effects=True, vmem_limit_bytes=48 * 2**20
        ),
        name="attention_layer",
    )(half_order, frame_ids, queries, keys, values, out_weight)


def solution(mesh):
    placed = (P("ctx", "head"), P("ctx", "head"), P("ctx", "head"), P(), P(), P("head", None))
    return jax.shard_map(
        per_device, mesh=mesh, in_specs=placed, out_specs=P("ctx", "head"), check_vma=False
    )
```

time: 417 us -> 87 us (0.21)
  waiting for transfers between devices: 223 us -> 0 us
  local copies, waits for them, and re-layouts: 90 us -> 6.54 us
  Pallas kernels: 0 us -> 80.2 us
  matrix products: 45 us -> 0 us
  other arithmetic: 22.6 us -> 0 us
  loops' own time: 20.2 us -> 0 us
  between operations: 13.2 us -> 0.02 us
    all_gather x2 -> x0, waiting for transfers between devices: 186 us -> none  [the longest x1 101 us: per_device(): key_rows = lax.all_gather(keys, 'ctx', axis=0, tiled=True)]
    pallas_call x0 -> x1, Pallas kernels: none -> 80.2 us  [per_device(): pl.pallas_call(kernel, out_shape=jax.ShapeDtypeStruct((ROWS, COLS), bf16)...]
    dynamic_slice x64 -> x0, local copies, waits for them, and re-layouts: 63.3 us -> none  [per_device(): lax.scan(one_tile, carried, (key_tiles, value_tiles, jnp.arange(tile_coun...]
    dot_general x65 -> x0, matrix products: 45 us -> none  [the longest x32 23.6 us: one_tile(): jnp.einsum('hqk,khd->hqd', weights.astype(jnp.bfloat16), value_tile, pref...]
    reduce_scatter x1 -> x0, waiting for transfers between devices: 35.4 us -> none  [per_device(): lax.psum_scatter(partial_value.astype(jnp.bfloat16), 'head', scatter_dime...]
    reshape x2 -> x0, local copies, waits for them, and re-layouts: 25.1 us -> none  [the longest x1 12.5 us: per_device(): key_tiles = key_rows.reshape(tile_count, tile_rows, heads_dev, HD)]
    another operation x1 -> x0, loops' own time: 20.2 us -> none  [per_device(): lax.scan(one_tile, carried, (key_tiles, value_tiles, jnp.arange(tile_coun...]
    reduce_sum x67 -> x0, other arithmetic: 14.4 us -> none  [the longest x32 9.65 us: one_tile(): totals = totals * shrink + jnp.sum(weights, axis=2)]
  transfers between devices with their start and end apart: 3 -> 0, of which waited for: 3 -> 0; matrix products, arithmetic and copies ran while one was open for 4% -> 0% of each run, Pallas kernels for 0% -> 0%
where the time goes in v1:
time: 87 us; the launch traced here: 86.8 us
  Pallas kernels  80.2 us (92%)
  local copies, waits for them, and re-layouts  6.54 us (8%)
    pallas_call x1, Pallas kernels, per_device(): pl.pallas_call(kernel, out_shape=jax.ShapeDtypeStruct((ROWS, COLS), bf16)...  80.2 us
    unnamed x13, local copies, waits for them, and re-layouts  6.54 us

profile of v1, /device:TPU:1, one launch (start us, length us, event | category | flops | bytes accessed | tf_op | source)
XLA Modules:
  0.0 86.8 jit_solution(12629776774567677034)
XLA Ops:
  0.0 0.0 copy-start
  0.0 1.6 %copy-done = bf16[256,4096]{1,0:T(8,128)(2,1)S(1)} copy-done((bf16[256,4096]{1,0:T(8,128)(2,1)S(1)}, bf16[256,4096]{1,0:T(8,128)(2,1)}, u32[]{:S(2)}) %copy-start) | copy-done | bytes 2097176
  1.6 0.0 copy-start.1
  1.6 0.9 %copy-done.1 = bf16[512,256]{1,0:T(8,128)(2,1)S(1)} copy-done((bf16[512,256]{1,0:T(8,128)(2,1)S(1)}, bf16[512,256]{1,0:T(8,128)(2,1)}, u32[]{:S(2)}) %copy-start.1) | copy-done | bytes 262168
  2.5 0.0 copy-start.2
  2.5 0.9 %copy-done.2 = bf16[512,256]{1,0:T(8,128)(2,1)S(1)} copy-done((bf16[512,256]{1,0:T(8,128)(2,1)S(1)}, bf16[512,256]{1,0:T(8,128)(2,1)}, u32[]{:S(2)}) %copy-start.2) | copy-done | bytes 262168
  3.5 0.0 copy-start.3
  3.5 0.9 %copy-done.3 = bf16[512,256]{1,0:T(8,128)(2,1)S(1)} copy-done((bf16[512,256]{1,0:T(8,128)(2,1)S(1)}, bf16[512,256]{1,0:T(8,128)(2,1)}, u32[]{:S(2)}) %copy-start.3) | copy-done | bytes 262168
  4.4 0.0 copy-start.4
  4.4 0.7 copy-done.4
  5.1 0.0 copy-start.5
  5.1 0.7 copy-done.5
  5.8 80.2 %attention_layer.1 = bf16[512,512]{1,0:T(8,128)(2,1)S(1)} custom-call(s32[64]{0:T(128)S(1)} %copy-done.4, s32[64]{0:T(128)S(1)} %copy-done.5, bf16[512,256]{1,0:T(8,128)(2,1)S(1)} %copy-done.1, bf16[512,256]{1,0:T(8,128)(2,1)S(1)} %copy-done.2, bf16[512,256]{1,0:T(8,128)(2,1)S(1)} %copy-done.3, bf16[256,4096]{1,0:T(8,128)(2,1)S(1)} %copy-done), custom_call_target="tpu_custom_call" | custom-call | tf_op jit(solution)/shard_map/attention_layer/pallas_call | solution.py:301
  86.0 0.8 copy.8
Async XLA Ops:
  0.0 1.6 %copy-start = (bf16[256,4096]{1,0:T(8,128)(2,1)S(1)}, bf16[256,4096]{1,0:T(8,128)(2,1)}, u32[]{:S(2)}) copy-start(bf16[256,4096]{1,0:T(8,128)(2,1)} %w_hbm.1) | copy-start | bytes 6291460
  1.6 0.9 %copy-start.1 = (bf16[512,256]{1,0:T(8,128)(2,1)S(1)}, bf16[512,256]{1,0:T(8,128)(2,1)}, u32[]{:S(2)}) copy-start(bf16[512,256]{1,0:T(8,128)(2,1)} %q_hbm.1) | copy-start | bytes 786436
  2.5 0.9 %copy-start.2 = (bf16[512,256]{1,0:T(8,128)(2,1)S(1)}, bf16[512,256]{1,0:T(8,128)(2,1)}, u32[]{:S(2)}) copy-start(bf16[512,256]{1,0:T(8,128)(2,1)} %k_hbm.1) | copy-start | bytes 786436
  3.5 0.9 %copy-start.3 = (bf16[512,256]{1,0:T(8,128)(2,1)S(1)}, bf16[512,256]{1,0:T(8,128)(2,1)}, u32[]{:S(2)}) copy-start(bf16[512,256]{1,0:T(8,128)(2,1)} %v_hbm.1) | copy-start | bytes 786436
  4.4 0.7 copy-start.4
  5.1 0.7 copy-start.5

commit v2 on v0

v2 whole, which is shorter than its diff:
```python
import math

import jax
import jax.numpy as jnp
from jax import lax
from jax.experimental import pallas as pl
from jax.experimental.pallas import tpu as pltpu
from jax.sharding import PartitionSpec as P

HD = 128
HALF = 256
ROWS = 512
NX, NY, NZ = 4, 4, 8
COLS = 512
SCALE = math.log2(math.e) / math.sqrt(HD)
HIDE = 2e30
LOWEST = -1e30
NT = (((1,), (1,)), ((), ()))
NN = (((1,), (0,)), ((), ()))


def kernel(
    order_ref, frames_ref, q_hbm, k_hbm, v_hbm, w_hbm, out_ref,
    q_buf, kv, acc, top, total, part_out, part_lse, part, lse, att, w_buf, out_acc,
    q_recv, kv_recv, part_recv, lse_recv, att_recv, w_recv,
    first_send, q_send, ring_send, side_send, w_send, part_send, lse_send, att_send, att_side_send,
):
    ctx, j = lax.axis_index("ctx"), lax.axis_index("head")
    z, x = ctx // NX, ctx % NX
    y, b = j // 2, j % 2
    k = z % 4

    def at(dz, core):
        return {"ctx": ((z + dz + 2 * NZ) % NZ) * NX + x, "head": y * 2 + core}

    side = at(0, 1 - b)
    x_up = {"ctx": z * NX + (x + 1) % NX, "head": j}
    x_down = {"ctx": z * NX + (x + NX - 1) % NX, "head": j}

    def remote(src, dst, send, recv, device):
        return pltpu.make_async_remote_copy(
            src_ref=src, dst_ref=dst, send_sem=send, recv_sem=recv,
            device_id=device, device_id_type=pl.DeviceIdType.MESH,
        )

    def arrived(ref, sem):
        pltpu.make_async_copy(ref, ref, sem).wait()

    def send_or_keep(keep, src, dst, send, recv, device):
        @pl.when(keep)
        def _():
            pltpu.make_async_copy(src, dst, recv).start()

        @pl.when(jnp.logical_not(keep))
        def _():
            remote(src, dst, send, recv, device).start()

    def sent_unless(keep, src, dst, send, recv, device):
        @pl.when(jnp.logical_not(keep))
        def _():
            remote(src, dst, send, recv, device).wait_send()

    def dist(i):
        return (z + NZ - 2 * b - i) % 4

    def kv_target(i):
        d = dist(i)
        two = jnp.where(z % 2 == 0, -2, 2)
        dz = jnp.where(d == 0, 0, jnp.where(d == 1, -1, jnp.where(d == 2, two, 1)))
        slot = jnp.where(d % 2 == 0, d // 2, (3 - d) // 2)
        return at(dz, d % 2), slot

    def own_head(i):
        return jnp.logical_and(dist(i) == 0, b == 0)

    barrier = pltpu.get_barrier_semaphore()

    def greet(device):
        pl.semaphore_signal(barrier, inc=1, device_id=device, device_id_type=pl.DeviceIdType.MESH)

    def greet_unless(keep, device):
        @pl.when(jnp.logical_not(keep))
        def _():
            greet(device)

    for device in [{"ctx": ctx, "head": (j + d) % (2 * NY)} for d in range(1, 2 * NY)] + [x_up, x_down]:
        greet(device)
    for i in range(2):
        greet_unless(own_head(i), at(-dist(i), dist(i) % 2))
        greet(at(-dist(i) - 4, dist(i) % 2))
    first_self = jnp.logical_and(b == 0, k < 2)
    for n in range(4):
        source = at(b + 2 * n, k // 2)
        same = at(b + 2 * n, b)
        if n == 0:
            greet_unless(first_self, source)
            greet_unless(b == 0, same)
        else:
            greet(source)
            greet(same)
    pl.semaphore_wait(
        barrier, 2 * NY - 1 + 2 + 12 - 2 * jnp.where(first_self, 1, 0) - jnp.where(b == 0, 1, 0)
    )

    def head_cols(i):
        return pl.ds(pl.multiple_of(i * HD, HD), HD)

    def kv_copy(i, what):
        device, slot = kv_target(i)
        src = (k_hbm, v_hbm)[what].at[:, head_cols(i)]
        return own_head(i), src, kv.at[slot, what], first_send.at[i, what], kv_recv.at[slot], device

    def q_copy(i, m):
        slot = dist(i) // 2 + 2 * m
        keep = jnp.logical_and(own_head(i), m == 0)
        device = at(-dist(i) - 4 * m, dist(i) % 2)
        return keep, q_hbm.at[:, head_cols(i)], q_buf.at[slot], q_send.at[i, m], q_recv.at[slot], device

    near_head = jnp.where(jnp.logical_or(dist(0) == 0, dist(0) == 3), 0, 1)
    heads = [near_head, 1 - near_head]
    nearer = [jnp.where(dist(i) < 2, 0, 1) for i in heads]
    for i in heads:
        for what in range(2):
            send_or_keep(*kv_copy(i, what))
    for i, m in zip(heads, nearer):
        send_or_keep(*q_copy(i, m))

    def w_copy(n):
        ry, other = n % NY, n // NY
        target = ((y + ry) % NY) * 2 + (1 - b if other else b)
        place = (NY - ry) % NY + NY * other
        src = w_hbm.at[:, pl.ds(pl.multiple_of(target * COLS, COLS), COLS)]
        if n == 0:
            return pltpu.make_async_copy(src, w_buf.at[0], w_recv.at[0])
        return remote(src, w_buf.at[place], w_send.at[n], w_recv.at[place], {"ctx": ctx, "head": target})

    acc[...] = jnp.zeros_like(acc)
    total[...] = jnp.zeros_like(total)
    top[...] = jnp.full_like(top, LOWEST)

    def ring_copy(e, later, sem, device):
        return remote(kv.at[e], kv.at[later], ring_send.at[sem], kv_recv.at[later], device)

    def side_copy(e):
        return remote(kv.at[e], kv.at[8 + e], side_send.at[e], kv_recv.at[8 + e], side)

    rings = [
        ring_copy(0, 2, 0, x_up), ring_copy(0, 3, 1, x_down),
        ring_copy(1, 4, 2, x_up), ring_copy(1, 5, 3, x_down),
        ring_copy(2, 6, 4, x_up), ring_copy(5, 7, 5, x_down),
    ]

    def take(e, forward=()):
        arrived(kv.at[e], kv_recv.at[e])
        for n in forward:
            rings[n].start()
        side_copy(e).start()

    take(0, (0, 1))
    take(1, (2, 3))
    for i, m in zip(heads, nearer):
        send_or_keep(*q_copy(i, 1 - m))
    for n in range(2 * NY):
        w_copy(n).start()

    def frame(c, h):
        return frames_ref[order_ref[2 * c + h]]

    def shard_of(core, rx, n):
        x_src = (x + rx) % NX
        even = jnp.where(n == 0, 0, jnp.where(z % 2 == 0, 2, -2))
        odd = jnp.where(n == 0, -1, 1)
        dz = jnp.where(core == 0, even, odd)
        return ((z + dz + NZ) % NZ) * NX + x_src

    def attend(tiles, g):
        q_frames = [frame(((z + b + 2 * (t // 2)) % NZ) * NX + x, t % 2) for t in tiles]
        rx_a = jnp.where(g == 0, 0, jnp.where(g == 3, 2, 3))
        rx_b = jnp.where(g == 0, 0, jnp.where(g == 3, 2, 1))
        n_a = jnp.where(g == 2, 1, 0)
        n_b = jnp.where(g == 1, 0, 1)

        def load(core):
            first = 8 * core + 2 * g
            keys = jnp.concatenate([kv[first, 0], kv[first + 1, 0]], axis=0)
            values = jnp.concatenate([kv[first, 1], kv[first + 1, 1]], axis=0)
            values = jnp.concatenate([values, jnp.ones_like(values)], axis=1)
            side_core = 1 - b if core else b
            shards = (shard_of(side_core, rx_a, n_a), shard_of(side_core, rx_b, n_b))
            return keys, values, [frame(c, h) for c in shards for h in range(2)]

        groups = [load(0), load(1)]

        def score(h, core):
            queries = q_buf[tiles[h] // 2, pl.ds(pl.multiple_of((tiles[h] % 2) * HALF, HALF), HALF), :]
            return lax.dot_general(queries, groups[core][0], NT, preferred_element_type=jnp.float32)

        def finish(h, core, scores):
            rows = pl.ds(pl.multiple_of(tiles[h] * HALF, HALF), HALF)
            hide = [jnp.where(f <= q_frames[h], 0.0, HIDE) for f in groups[core][2]]
            best = None
            for a in range(4):
                peak = jnp.maximum(
                    scores[:, a * HALF : a * HALF + HD], scores[:, a * HALF + HD : (a + 1) * HALF]
                ) - hide[a]
                best = peak if best is None else jnp.maximum(best, peak)
            old = top[rows, :]
            new = jnp.maximum(old, jnp.max(best, axis=1, keepdims=True) * SCALE)
            weights = []
            for a in range(4):
                floor = new + hide[a]
                for s in range(2):
                    col = a * HALF + s * HD
                    weights.append(jnp.exp2(scores[:, col : col + HD] * SCALE - floor).astype(jnp.bfloat16))
            weights = jnp.concatenate(weights, axis=1)
            product = lax.dot_general(weights, groups[core][1], NN, preferred_element_type=jnp.float32)
            shrink = jnp.exp2(old - new)
            acc[rows, :] = acc[rows, :] * shrink + product[:, :HD]
            total[rows, :] = total[rows, :] * shrink + product[:, HD:]
            top[rows, :] = new

        steps = [(0, 0), (1, 0), (0, 1), (1, 1)]
        scores = score(*steps[0])
        for s, here in enumerate(steps):
            following = score(*steps[s + 1]) if s < 3 else None
            finish(*here, scores)
            scores = following

    lanes = lax.broadcasted_iota(jnp.int32, (HD, HD), 1)
    diagonal = lanes == lax.broadcasted_iota(jnp.int32, (HD, HD), 0)

    def part_copies(t):
        device = at(b + 2 * (t // 2), b)
        quarter, m = t % 4, t // 4
        keep = jnp.logical_and(t < 2, b == 0)
        return (
            (keep, part_out.at[t], part.at[quarter, m], part_send.at[t], part_recv.at[quarter, m], device),
            (keep, part_lse.at[t], lse.at[quarter, m], lse_send.at[t], lse_recv.at[quarter, m], device),
        )

    def close(t):
        rows = pl.ds(pl.multiple_of(t * HALF, HALF), HALF)
        sums = jnp.maximum(total[rows, :], 0.5)
        part_out[t] = (acc[rows, :] / sums).astype(jnp.bfloat16)
        logs = top[rows, :] + jnp.log2(sums)
        for r in range(2):
            line = jnp.where(diagonal, logs[r * HD : (r + 1) * HD, :], 0.0)
            part_lse[t, r : r + 1, :] = jnp.sum(line, axis=0, keepdims=True)
        for copy in part_copies(t):
            send_or_keep(*copy)

    def y_copy(quarter, ry):
        device = {"ctx": ctx, "head": ((y + ry) % NY) * 2 + b}
        there = (NY - ry) % NY
        return remote(
            att.at[0, quarter, 0], att.at[0, quarter, there], att_send.at[quarter, ry - 1],
            att_recv.at[0, quarter, there], device,
        )

    def att_side(quarter, ry):
        return remote(
            att.at[0, quarter, ry], att.at[1, quarter, ry], att_side_send.at[quarter, ry],
            att_recv.at[1, quarter, ry], side,
        )

    def merge(quarter):
        for m in range(2):
            arrived(part.at[quarter, m], part_recv.at[quarter, m])
            arrived(lse.at[quarter, m], lse_recv.at[quarter, m])
        for r in range(2):
            rows = pl.ds(r * HD, HD)
            logs = []
            for m in range(2):
                line = jnp.broadcast_to(lse[quarter, m, r : r + 1, :], (HD, HD))
                logs.append(jnp.sum(jnp.where(diagonal, line, 0.0), axis=1, keepdims=True))
            high = jnp.maximum(logs[0], logs[1])
            shares = [jnp.exp2(log - high) for log in logs]
            whole = shares[0] + shares[1]
            mixed = sum(
                part[quarter, m, rows, :].astype(jnp.float32) * (shares[m] / whole) for m in range(2)
            )
            att[0, quarter, 0, rows, :] = mixed.astype(jnp.bfloat16)
        for ry in (1, 3, 2):
            y_copy(quarter, ry).start()
        att_side(quarter, 0).start()

    def step(i, carry):
        opening = i < 4
        n = jnp.where(i == 0, 0, jnp.where(i == 1, 3, i - 1))
        quarter = jnp.where(
            i < 8, i % 4, jnp.where(i < 10, i - 6, jnp.where(i < 14, (i - 10) // 2, i - 12))
        )
        g = jnp.where(
            i < 8, i // 4, jnp.where(i < 10, 2, jnp.where(i < 14, 2 + i % 2, 3))
        )
        tiles = (jnp.where(opening, 2 * n, quarter), jnp.where(opening, 2 * n + 1, quarter + 4))

        @pl.when(opening)
        def _():
            arrived(q_buf.at[n], q_recv.at[n])

        @pl.when(i == 0)
        def _():
            for e in range(8, 10):
                arrived(kv.at[e], kv_recv.at[e])

        @pl.when(i == 1)
        def _():
            take(2, (4,))
            take(3)

        @pl.when(i == 3)
        def _():
            take(4)
            take(5, (5,))

        @pl.when(i == 4)
        def _():
            for e in range(10, 12):
                arrived(kv.at[e], kv_recv.at[e])

        @pl.when(i == 8)
        def _():
            for e in range(12, 14):
                arrived(kv.at[e], kv_recv.at[e])

        @pl.when(i == 9)
        def _():
            for e in range(6, 8):
                take(e)

        @pl.when(i == 11)
        def _():
            for e in range(14, 16):
                arrived(kv.at[e], kv_recv.at[e])

        @pl.when(i == 14)
        def _():
            merge(0)

        attend(tiles, g)

        @pl.when(jnp.logical_or(i == 11, i >= 13))
        def _():
            close(tiles[0])
            close(tiles[1])

        return carry

    lax.fori_loop(0, 16, step, 0)

    def project(quarter):
        slot, h = quarter // 2, quarter % 2
        rows, weights = [], []
        for core in range(2):
            for ry in range(NY):
                t = 1 - b if core else b
                head = (z + NZ - t - 2 * slot) % 4
                place = ry + jnp.where(head // 2 == b, 0, NY)
                rows.append(att[core, quarter, ry])
                weights.append(w_buf[place, pl.ds(pl.multiple_of((head % 2) * HD, HD), HD), :])
        product = lax.dot_general(
            jnp.concatenate(rows, axis=1), jnp.concatenate(weights, axis=0), NN,
            preferred_element_type=jnp.float32,
        )
        here = pl.ds(h * HALF, HALF)
        if slot == 0:
            out_acc[here, :] = product
        else:
            out_ref[here, :] = (out_acc[here, :] + product).astype(out_ref.dtype)

    def gather(quarter):
        for ry in (1, 3, 2):
            arrived(att.at[0, quarter, ry], att_recv.at[0, quarter, ry])
            att_side(quarter, ry).start()

    def finish(quarter):
        for ry in range(NY):
            arrived(att.at[1, quarter, ry], att_recv.at[1, quarter, ry])
        project(quarter)

    merge(1)
    gather(0)
    merge(2)
    for n in range(2 * NY):
        arrived(w_buf.at[n], w_recv.at[n])
    finish(0)
    merge(3)
    for quarter in range(1, 4):
        gather(quarter)
        finish(quarter)

    for i in range(2):
        for what in range(2):
            sent_unless(*kv_copy(i, what))
            sent_unless(*q_copy(i, what))
    for n in range(1, 2 * NY):
        w_copy(n).wait_send()
    for copy in rings:
        copy.wait_send()
    for e in range(8):
        side_copy(e).wait_send()
    for t in range(8):
        for copy in part_copies(t):
            sent_unless(*copy)
    for quarter in range(4):
        for ry in range(1, NY):
            y_copy(quarter, ry).wait_send()
        for ry in range(NY):
            att_side(quarter, ry).wait_send()


def per_device(queries, keys, values, frame_ids, half_order, out_weight):
    hbm = pl.BlockSpec(memory_space=pltpu.HBM)
    smem = pl.BlockSpec(memory_space=pltpu.SMEM)
    bf16, f32 = jnp.bfloat16, jnp.float32
    dma = pltpu.SemaphoreType.DMA
    return pl.pallas_call(
        kernel,
        out_shape=jax.ShapeDtypeStruct((ROWS, COLS), bf16),
        in_specs=[smem, smem, hbm, hbm, hbm, hbm],
        out_specs=pl.BlockSpec(memory_space=pltpu.VMEM),
        scratch_shapes=[
            pltpu.VMEM((4, ROWS, HD), bf16),
            pltpu.VMEM((16, 2, ROWS, HD), bf16),
            pltpu.VMEM((4 * ROWS, HD), f32),
            pltpu.VMEM((4 * ROWS, HD), f32),
            pltpu.VMEM((4 * ROWS, HD), f32),
            pltpu.VMEM((8, HALF, HD), bf16),
            pltpu.VMEM((8, 8, HD), f32),
            pltpu.VMEM((4, 2, HALF, HD), bf16),
            pltpu.VMEM((4, 2, 8, HD), f32),
            pltpu.VMEM((2, 4, NY, HALF, HD), bf16),
            pltpu.VMEM((2 * NY, 2 * HD, COLS), bf16),
            pltpu.VMEM((ROWS, COLS), f32),
            dma((4,)), dma((16,)), dma((4, 2)), dma((4, 2)), dma((2, 4, NY)), dma((2 * NY,)),
            dma((2, 2)), dma((2, 2)), dma((6,)), dma((8,)), dma((2 * NY,)), dma((8,)), dma((8,)),
            dma((4, NY - 1)), dma((4, NY)),
        ],
        compiler_params=pltpu.CompilerParams(
            collective_id=0, has_side_effects=True, vmem_limit_bytes=62 * 2**20
        ),
        name="attention_layer",
    )(half_order, frame_ids, queries, keys, values, out_weight)


def solution(mesh):
    placed = (P("ctx", "head"), P("ctx", "head"), P("ctx", "head"), P(), P(), P("head", None))
    return jax.shard_map(
        per_device, mesh=mesh, in_specs=placed, out_specs=P("ctx", "head"), check_vma=False
    )
```

time: 417 us -> 74.1 us (0.18)
  waiting for transfers between devices: 223 us -> 0 us
  local copies, waits for them, and re-layouts: 90 us -> 1.87 us
  Pallas kernels: 0 us -> 71.2 us
  matrix products: 45 us -> 0 us
  other arithmetic: 22.6 us -> 0 us
  loops' own time: 20.2 us -> 0 us
  between operations: 13.2 us -> 0.01 us
    all_gather x2 -> x0, waiting for transfers between devices: 186 us -> none  [the longest x1 101 us: per_device(): key_rows = lax.all_gather(keys, 'ctx', axis=0, tiled=True)]
    pallas_call x0 -> x1, Pallas kernels: none -> 71.2 us  [per_device(): pl.pallas_call(kernel, out_shape=jax.ShapeDtypeStruct((ROWS, COLS), bf16)...]
    dynamic_slice x64 -> x0, local copies, waits for them, and re-layouts: 63.3 us -> none  [per_device(): lax.scan(one_tile, carried, (key_tiles, value_tiles, jnp.arange(tile_coun...]
    dot_general x65 -> x0, matrix products: 45 us -> none  [the longest x32 23.6 us: one_tile(): jnp.einsum('hqk,khd->hqd', weights.astype(jnp.bfloat16), value_tile, pref...]
    reduce_scatter x1 -> x0, waiting for transfers between devices: 35.4 us -> none  [per_device(): lax.psum_scatter(partial_value.astype(jnp.bfloat16), 'head', scatter_dime...]
    reshape x2 -> x0, local copies, waits for them, and re-layouts: 25.1 us -> none  [the longest x1 12.5 us: per_device(): key_tiles = key_rows.reshape(tile_count, tile_rows, heads_dev, HD)]
    another operation x1 -> x0, loops' own time: 20.2 us -> none  [per_device(): lax.scan(one_tile, carried, (key_tiles, value_tiles, jnp.arange(tile_coun...]
    reduce_sum x67 -> x0, other arithmetic: 14.4 us -> none  [the longest x32 9.65 us: one_tile(): totals = totals * shrink + jnp.sum(weights, axis=2)]
  transfers between devices with their start and end apart: 3 -> 0, of which waited for: 3 -> 0; matrix products, arithmetic and copies ran while one was open for 4% -> 0% of each run, Pallas kernels for 0% -> 0%
where the time goes in v2:
time: 74.1 us; the launch traced here: 73.1 us
  Pallas kernels  71.2 us (96%)
  local copies, waits for them, and re-layouts  1.87 us (3%)
    pallas_call x1, Pallas kernels, per_device(): pl.pallas_call(kernel, out_shape=jax.ShapeDtypeStruct((ROWS, COLS), bf16)...  71.2 us
    unnamed x1, local copies, waits for them, and re-layouts  1.87 us

profile of v2, /device:TPU:1, one launch (start us, length us, event | category | flops | bytes accessed | tf_op | source)
XLA Modules:
  0.0 73.1 jit_solution(14397764177664039489)
XLA Ops:
  0.0 71.2 %attention_layer.1 = bf16[512,512]{1,0:T(8,128)(2,1)} custom-call(s32[64]{0:T(128)} %order_ref.1, s32[64]{0:T(128)} %frames_ref.1, bf16[512,256]{1,0:T(8,128)(2,1)} %q_hbm.1, bf16[512,256]{1,0:T(8,128)(2,1)} %k_hbm.1, bf16[512,256]{1,0:T(8,128)(2,1)} %v_hbm.1, bf16[256,4096]{1,0:T(8,128)(2,1)} %w_hbm.1), custom_call_target="tpu_custom_call" | custom-call | tf_op jit(solution)/shard_map/attention_layer/pallas_call | solution.py:418
  71.2 1.9 %copy.8 = bf16[512,512]{1,0:T(8,128)(2,1)} copy(bf16[512,512]{1,0:T(8,128)(2,1)} %attention_layer.1) | data formatting | bytes 1048576

commit v3 on v2

--- a/solution.py
+++ b/solution.py
@@ -15,15 +15,24 @@
 SCALE = math.log2(math.e) / math.sqrt(HD)
 HIDE = 2e30
 LOWEST = -1e30
+LOG_ROWS = 16
 NT = (((1,), (1,)), ((), ()))
 NN = (((1,), (0,)), ((), ()))
+SCHEDULE = [[(t, e + d) for t, d in ((0, 0), (1, 0), (1, 1), (6, 0), (7, 0), (7, 1))] for e in (0, 2, 4)] + [
+    [(2, 0), (3, 0), (3, 1), (2, 2), (3, 2), (3, 3)],
+    [(2, 4), (3, 4), (3, 5), (2, 6), (3, 6), (3, 7)],
+    [(6, 6), (7, 6), (4, 0), (7, 7), (4, 2), (4, 4)],
+    [(4, 6), (5, 0), (0, 6), (5, 1), (5, 2), (5, 3)],
+    [(5, 4), (1, 6), (5, 5), (1, 7), (5, 6), (5, 7)],
+]
 
 
 def kernel(
     order_ref, frames_ref, q_hbm, k_hbm, v_hbm, w_hbm, out_ref,
-    q_buf, kv, acc, top, total, part_out, part_lse, part, lse, att, w_buf, out_acc,
-    q_recv, kv_recv, part_recv, lse_recv, att_recv, w_recv,
-    first_send, q_send, ring_send, side_send, w_send, part_send, lse_send, att_send, att_side_send,
+    q_buf, kv, acc, top, total, part_out, part, att, w_buf, out_acc,
+    key_frames, query_frames, beyond,
+    q_recv, kv_recv, part_recv, att_recv, w_recv,
+    first_send, q_send, ring_send, side_send, w_send, part_send, att_send, att_side_send,
 ):
     ctx, j = lax.axis_index("ctx"), lax.axis_index("head")
     z, x = ctx // NX, ctx % NX
@@ -114,16 +123,22 @@
         slot = dist(i) // 2 + 2 * m
         keep = jnp.logical_and(own_head(i), m == 0)
         device = at(-dist(i) - 4 * m, dist(i) % 2)
-        return keep, q_hbm.at[:, head_cols(i)], q_buf.at[slot], q_send.at[i, m], q_recv.at[slot], device
+        return keep, q_hbm.at[:, head_cols(i)], q_buf.at[pl.ds(pl.multiple_of(slot * ROWS, ROWS), ROWS)], q_send.at[i, m], q_recv.at[slot], device
 
     near_head = jnp.where(jnp.logical_or(dist(0) == 0, dist(0) == 3), 0, 1)
     heads = [near_head, 1 - near_head]
     nearer = [jnp.where(dist(i) < 2, 0, 1) for i in heads]
+    def near_queries(when):
+        for i, m in zip(heads, nearer):
+            @pl.when((dist(i) < 2) == when)
+            def _():
+                send_or_keep(*q_copy(i, m))
+
+    near_queries(True)
     for i in heads:
         for what in range(2):
             send_or_keep(*kv_copy(i, what))
-    for i, m in zip(heads, nearer):
-        send_or_keep(*q_copy(i, m))
+    near_queries(False)
 
     def w_copy(n):
         ry, other = n % NY, n // NY
@@ -157,9 +172,23 @@
         side_copy(e).start()
 
     take(0, (0, 1))
-    take(1, (2, 3))
-    for i, m in zip(heads, nearer):
-        send_or_keep(*q_copy(i, 1 - m))
+
+    @pl.when(b == 0)
+    def _():
+        take(2, (4,))
+
+    @pl.when(b == 1)
+    def _():
+        take(1, (2, 3))
+
+    def far_queries(when):
+        for i, m in zip(heads, nearer):
+            @pl.when((dist(i) >= 2) == when)
+            def _():
+                remote(*q_copy(i, 1 - m)[1:]).start()
+
+    far_queries(True)
+
     for n in range(2 * NY):
         w_copy(n).start()
 
@@ -173,33 +202,41 @@
         dz = jnp.where(core == 0, even, odd)
         return ((z + dz + NZ) % NZ) * NX + x_src
 
-    def attend(tiles, g):
-        q_frames = [frame(((z + b + 2 * (t // 2)) % NZ) * NX + x, t % 2) for t in tiles]
-        rx_a = jnp.where(g == 0, 0, jnp.where(g == 3, 2, 3))
-        rx_b = jnp.where(g == 0, 0, jnp.where(g == 3, 2, 1))
-        n_a = jnp.where(g == 2, 1, 0)
-        n_b = jnp.where(g == 1, 0, 1)
-
-        def load(core):
-            first = 8 * core + 2 * g
-            keys = jnp.concatenate([kv[first, 0], kv[first + 1, 0]], axis=0)
-            values = jnp.concatenate([kv[first, 1], kv[first + 1, 1]], axis=0)
+    def shard_of_piece(core, e):
+        rx = 0 if e < 2 else 2 if e >= 6 else 3 - 2 * (e % 2)
+        return shard_of(core, rx, e if e < 2 else e - 6 if e >= 6 else (e - 2) // 2)
+
+    middle = order_ref.shape[0] // 2
+    places, founds = [0, 0, 0], [0, 0, 0]
+    for e in range(8):
+        for core in range(2):
+            c = shard_of_piece(1 - b if core else b, e)
+            for h in range(2):
+                key_frames[2 * (8 * core + e) + h] = frame(c, h)
+            upper = order_ref[2 * c + 1]
+            for p in range(3):
+                here = jnp.where(upper == middle + p, 1, 0)
+                places[p] += here * (8 * core + e)
+                founds[p] += here
+    for p in range(3):
+        beyond[p] = places[p]
+        beyond[3 + p] = founds[p]
+    for n in range(4):
+        for h in range(2):
+            query_frames[2 * n + h] = frame(((z + b + 2 * n) % NZ) * NX + x, h)
+
+    def meet(steps):
+        def score(t, load, hide):
+            queries = q_buf[pl.ds(pl.multiple_of(t * HALF, HALF), HALF), :]
+            return lax.dot_general(queries, load(0), NT, preferred_element_type=jnp.float32)
+
+        def finish(t, load, hide, scores):
+            values = load(1)
             values = jnp.concatenate([values, jnp.ones_like(values)], axis=1)
-            side_core = 1 - b if core else b
-            shards = (shard_of(side_core, rx_a, n_a), shard_of(side_core, rx_b, n_b))
-            return keys, values, [frame(c, h) for c in shards for h in range(2)]
-
-        groups = [load(0), load(1)]
-
-        def score(h, core):
-            queries = q_buf[tiles[h] // 2, pl.ds(pl.multiple_of((tiles[h] % 2) * HALF, HALF), HALF), :]
-            return lax.dot_general(queries, groups[core][0], NT, preferred_element_type=jnp.float32)
-
-        def finish(h, core, scores):
-            rows = pl.ds(pl.multiple_of(tiles[h] * HALF, HALF), HALF)
-            hide = [jnp.where(f <= q_frames[h], 0.0, HIDE) for f in groups[core][2]]
+            rows = pl.ds(pl.multiple_of(t * HALF, HALF), HALF)
+            hide = [jnp.where(hidden, HIDE, 0.0) for hidden in hide]
             best = None
-            for a in range(4):
+            for a in range(len(hide)):
                 peak = jnp.maximum(
                     scores[:, a * HALF : a * HALF + HD], scores[:, a * HALF + HD : (a + 1) * HALF]
                 ) - hide[a]
@@ -207,47 +244,80 @@
             old = top[rows, :]
             new = jnp.maximum(old, jnp.max(best, axis=1, keepdims=True) * SCALE)
             weights = []
-            for a in range(4):
+            for a in range(len(hide)):
                 floor = new + hide[a]
-                for s in range(2):
-                    col = a * HALF + s * HD
+                for half in range(2):
+                    col = a * HALF + half * HD
                     weights.append(jnp.exp2(scores[:, col : col + HD] * SCALE - floor).astype(jnp.bfloat16))
             weights = jnp.concatenate(weights, axis=1)
-            product = lax.dot_general(weights, groups[core][1], NN, preferred_element_type=jnp.float32)
+            product = lax.dot_general(weights, values, NN, preferred_element_type=jnp.float32)
             shrink = jnp.exp2(old - new)
             acc[rows, :] = acc[rows, :] * shrink + product[:, :HD]
             total[rows, :] = total[rows, :] * shrink + product[:, HD:]
             top[rows, :] = new
 
-        steps = [(0, 0), (1, 0), (0, 1), (1, 1)]
         scores = score(*steps[0])
         for s, here in enumerate(steps):
-            following = score(*steps[s + 1]) if s < 3 else None
+            following = score(*steps[s + 1]) if s + 1 < len(steps) else None
             finish(*here, scores)
             scores = following
 
+    def keys_step(t, e, low):
+        blocks = []
+        for a in range(4):
+            piece = jnp.where(low == 1, 8 * (a % 2) + a // 2 + e, 8 * (a // 2) + e)
+            blocks.append((piece, (1 - low) * (a % 2)))
+
+        def load(what):
+            return jnp.concatenate(
+                [
+                    kv[piece, what, pl.ds(pl.multiple_of(half * HALF, HALF), HALF), :]
+                    for piece, half in blocks
+                ],
+                axis=0,
+            )
+
+        q_frame = query_frames[t]
+        return t, load, [key_frames[2 * piece + half] > q_frame for piece, half in blocks]
+
+    def across_middle(tiles):
+        def load(what):
+            return jnp.concatenate([kv[beyond[p], what, pl.ds(HALF, HALF), :] for p in range(3)], axis=0)
+
+        steps = []
+        for t in tiles:
+            low = query_frames[t]
+            hide = [
+                jnp.logical_or(beyond[3 + p] == 0, frames_ref[middle + p] > low) for p in range(3)
+            ]
+            steps.append((t, load, hide))
+        meet(steps)
+
     lanes = lax.broadcasted_iota(jnp.int32, (HD, HD), 1)
+    log_row = lax.broadcasted_iota(jnp.int32, (LOG_ROWS, HD), 0)
     diagonal = lanes == lax.broadcasted_iota(jnp.int32, (HD, HD), 0)
 
-    def part_copies(t):
+    def part_copy(t):
         device = at(b + 2 * (t // 2), b)
         quarter, m = t % 4, t // 4
         keep = jnp.logical_and(t < 2, b == 0)
-        return (
-            (keep, part_out.at[t], part.at[quarter, m], part_send.at[t], part_recv.at[quarter, m], device),
-            (keep, part_lse.at[t], lse.at[quarter, m], lse_send.at[t], lse_recv.at[quarter, m], device),
-        )
+        return keep, part_out.at[t], part.at[quarter, m], part_send.at[t], part_recv.at[quarter, m], device
 
     def close(t):
         rows = pl.ds(pl.multiple_of(t * HALF, HALF), HALF)
         sums = jnp.maximum(total[rows, :], 0.5)
-        part_out[t] = (acc[rows, :] / sums).astype(jnp.bfloat16)
+        part_out[t, pl.ds(0, HALF), :] = (acc[rows, :] / sums).astype(jnp.bfloat16)
         logs = top[rows, :] + jnp.log2(sums)
+        tail = jnp.zeros((LOG_ROWS, HD), jnp.float32)
         for r in range(2):
             line = jnp.where(diagonal, logs[r * HD : (r + 1) * HD, :], 0.0)
-            part_lse[t, r : r + 1, :] = jnp.sum(line, axis=0, keepdims=True)
-        for copy in part_copies(t):
-            send_or_keep(*copy)
+            rest = jnp.sum(line, axis=0, keepdims=True)
+            for term in range(3):
+                rounded = rest.astype(jnp.bfloat16).astype(jnp.float32)
+                tail = jnp.where(log_row == 2 * term + r, rounded, tail)
+                rest = rest - rounded
+        part_out[t, pl.ds(HALF, LOG_ROWS), :] = tail.astype(jnp.bfloat16)
+        send_or_keep(*part_copy(t))
 
     def y_copy(quarter, ry):
         device = {"ctx": ctx, "head": ((y + ry) % NY) * 2 + b}
@@ -266,12 +336,13 @@
     def merge(quarter):
         for m in range(2):
             arrived(part.at[quarter, m], part_recv.at[quarter, m])
-            arrived(lse.at[quarter, m], lse_recv.at[quarter, m])
+        tails = [part[quarter, m, pl.ds(HALF, LOG_ROWS), :].astype(jnp.float32) for m in range(2)]
         for r in range(2):
             rows = pl.ds(r * HD, HD)
             logs = []
             for m in range(2):
-                line = jnp.broadcast_to(lse[quarter, m, r : r + 1, :], (HD, HD))
+                line = sum(tails[m][2 * term + r : 2 * term + r + 1, :] for term in range(3))
+                line = jnp.broadcast_to(line, (HD, HD))
                 logs.append(jnp.sum(jnp.where(diagonal, line, 0.0), axis=1, keepdims=True))
             high = jnp.maximum(logs[0], logs[1])
             shares = [jnp.exp2(log - high) for log in logs]
@@ -284,70 +355,62 @@
             y_copy(quarter, ry).start()
         att_side(quarter, 0).start()
 
+    def from_side(*pieces):
+        for e in pieces:
+            arrived(kv.at[8 + e], kv_recv.at[8 + e])
+
     def step(i, carry):
-        opening = i < 4
-        n = jnp.where(i == 0, 0, jnp.where(i == 1, 3, i - 1))
-        quarter = jnp.where(
-            i < 8, i % 4, jnp.where(i < 10, i - 6, jnp.where(i < 14, (i - 10) // 2, i - 12))
+        def now(key):
+            return sum(jnp.where(i == item, entry, 0) for item, entry in enumerate(key) if entry)
+
+        def event(when, act, *args):
+            @pl.when(when)
+            def _():
+                act(*args)
+
+        first_core, second_core = b == 0, b == 1
+        event(jnp.logical_and(i == 0, first_core), take, 1, (2, 3))
+        event(i == 0, lambda: [arrived(q_buf.at[pl.ds(n * ROWS, ROWS)], q_recv.at[n]) for n in (0, 3)])
+        event(i == 0, far_queries, False)
+        event(jnp.logical_and(i == 0, second_core), take, 2, (4,))
+        event(i == 0, take, 3)
+        event(i == 0, from_side, 0, 1)
+        event(i == 1, take, 5, (5,))
+        event(i == 1, take, 4)
+        event(i == 1, from_side, 2, 3)
+        event(i == 2, take, 6)
+        event(i == 2, from_side, 4, 5)
+        event(i == 3, lambda: arrived(q_buf.at[pl.ds(ROWS, ROWS)], q_recv.at[1]))
+        event(i == 3, take, 7)
+        event(i == 4, from_side, 6, 7)
+        event(i == 5, lambda: arrived(q_buf.at[pl.ds(2 * ROWS, ROWS)], q_recv.at[2]))
+
+        event(i == 7, merge, 2)
+        event(i == 7, merge, 3)
+
+        meet(
+            [
+                keys_step(
+                    now([item[s][0] for item in SCHEDULE]),
+                    now([item[s][1] for item in SCHEDULE]),
+                    now([1 - item[s][0] % 2 for item in SCHEDULE]),
+                )
+                for s in range(6)
+            ]
         )
-        g = jnp.where(
-            i < 8, i // 4, jnp.where(i < 10, 2, jnp.where(i < 14, 2 + i % 2, 3))
-        )
-        tiles = (jnp.where(opening, 2 * n, quarter), jnp.where(opening, 2 * n + 1, quarter + 4))
-
-        @pl.when(opening)
+
+        event(i == 4, lambda: across_middle([2]))
+        event(i == 5, lambda: across_middle([6]))
+        event(i == 6, lambda: across_middle([4, 0]))
+
+        @pl.when(i >= 4)
         def _():
-            arrived(q_buf.at[n], q_recv.at[n])
-
-        @pl.when(i == 0)
-        def _():
-            for e in range(8, 10):
-                arrived(kv.at[e], kv_recv.at[e])
-
-        @pl.when(i == 1)
-        def _():
-            take(2, (4,))
-            take(3)
-
-        @pl.when(i == 3)
-        def _():
-            take(4)
-            take(5, (5,))
-
-        @pl.when(i == 4)
-        def _():
-            for e in range(10, 12):
-                arrived(kv.at[e], kv_recv.at[e])
-
-        @pl.when(i == 8)
-        def _():
-            for e in range(12, 14):
-                arrived(kv.at[e], kv_recv.at[e])
-
-        @pl.when(i == 9)
-        def _():
-            for e in range(6, 8):
-                take(e)
-
-        @pl.when(i == 11)
-        def _():
-            for e in range(14, 16):
-                arrived(kv.at[e], kv_recv.at[e])
-
-        @pl.when(i == 14)
-        def _():
-            merge(0)
-
-        attend(tiles, g)
-
-        @pl.when(jnp.logical_or(i == 11, i >= 13))
-        def _():
-            close(tiles[0])
-            close(tiles[1])
+            close(now((0, 0, 0, 0, 2, 6, 4, 5)))
+            close(now((0, 0, 0, 0, 3, 7, 0, 1)))
 
         return carry
 
-    lax.fori_loop(0, 16, step, 0)
+    lax.fori_loop(0, 8, step, 0)
 
     def project(quarter):
         slot, h = quarter // 2, quarter % 2
@@ -364,7 +427,7 @@
             preferred_element_type=jnp.float32,
         )
         here = pl.ds(h * HALF, HALF)
-        if slot == 0:
+        if slot == 1:
             out_acc[here, :] = product
         else:
             out_ref[here, :] = (out_acc[here, :] + product).astype(out_ref.dtype)
@@ -378,17 +441,6 @@
         for ry in range(NY):
             arrived(att.at[1, quarter, ry], att_recv.at[1, quarter, ry])
         project(quarter)
-
-    merge(1)
-    gather(0)
-    merge(2)
-    for n in range(2 * NY):
-        arrived(w_buf.at[n], w_recv.at[n])
-    finish(0)
-    merge(3)
-    for quarter in range(1, 4):
-        gather(quarter)
-        finish(quarter)
 
     for i in range(2):
         for what in range(2):
@@ -400,9 +452,20 @@
         copy.wait_send()
     for e in range(8):
         side_copy(e).wait_send()
+    for n in range(2 * NY):
+        arrived(w_buf.at[n], w_recv.at[n])
+    merge(0)
+    gather(2)
+    gather(3)
+    finish(2)
+    merge(1)
+    finish(3)
+    gather(0)
+    gather(1)
+    finish(0)
+    finish(1)
     for t in range(8):
-        for copy in part_copies(t):
-            sent_unless(*copy)
+        sent_unless(*part_copy(t))
     for quarter in range(4):
         for ry in range(1, NY):
             y_copy(quarter, ry).wait_send()
@@ -421,20 +484,21 @@
         in_specs=[smem, smem, hbm, hbm, hbm, hbm],
         out_specs=pl.BlockSpec(memory_space=pltpu.VMEM),
         scratch_shapes=[
-            pltpu.VMEM((4, ROWS, HD), bf16),
+            pltpu.VMEM((4 * ROWS, HD), bf16),
             pltpu.VMEM((16, 2, ROWS, HD), bf16),
             pltpu.VMEM((4 * ROWS, HD), f32),
             pltpu.VMEM((4 * ROWS, HD), f32),
             pltpu.VMEM((4 * ROWS, HD), f32),
-            pltpu.VMEM((8, HALF, HD), bf16),
-            pltpu.VMEM((8, 8, HD), f32),
-            pltpu.VMEM((4, 2, HALF, HD), bf16),
-            pltpu.VMEM((4, 2, 8, HD), f32),
+            pltpu.VMEM((8, HALF + LOG_ROWS, HD), bf16),
+            pltpu.VMEM((4, 2, HALF + LOG_ROWS, HD), bf16),
             pltpu.VMEM((2, 4, NY, HALF, HD), bf16),
             pltpu.VMEM((2 * NY, 2 * HD, COLS), bf16),
             pltpu.VMEM((ROWS, COLS), f32),
-            dma((4,)), dma((16,)), dma((4, 2)), dma((4, 2)), dma((2, 4, NY)), dma((2 * NY,)),
-            dma((2, 2)), dma((2, 2)), dma((6,)), dma((8,)), dma((2 * NY,)), dma((8,)), dma((8,)),
+            pltpu.SMEM((32,), jnp.int32),
+            pltpu.SMEM((8,), jnp.int32),
+            pltpu.SMEM((6,), jnp.int32),
+            dma((4,)), dma((16,)), dma((4, 2)), dma((2, 4, NY)), dma((2 * NY,)),
+            dma((2, 2)), dma((2, 2)), dma((6,)), dma((8,)), dma((2 * NY,)), dma((8,)),
             dma((4, NY - 1)), dma((4, NY)),
         ],
         compiler_params=pltpu.CompilerParams(

time: 74.1 us -> 73.7 us (level)
  the two profiles are of different devices: /device:TPU:1 before, /device:TPU:89 now
where the time goes in v3:
time: 73.7 us; the launch traced here: 73.5 us
  Pallas kernels  71.7 us (97%)
  local copies, waits for them, and re-layouts  1.87 us (3%)
    pallas_call x1, Pallas kernels, per_device(): pl.pallas_call(kernel, out_shape=jax.ShapeDtypeStruct((ROWS, COLS), bf16)...  71.7 us
    unnamed x1, local copies, waits for them, and re-layouts  1.87 us

profile of v3, /device:TPU:89, one launch (start us, length us, event | category | flops | bytes accessed | tf_op | source)
XLA Modules:
  0.0 73.5 jit_solution(14298158692245762481)
XLA Ops:
  0.0 71.7 %attention_layer.1 = bf16[512,512]{1,0:T(8,128)(2,1)} custom-call(s32[64]{0:T(128)} %order_ref.1, s32[64]{0:T(128)} %frames_ref.1, bf16[512,256]{1,0:T(8,128)(2,1)} %q_hbm.1, bf16[512,256]{1,0:T(8,128)(2,1)} %k_hbm.1, bf16[512,256]{1,0:T(8,128)(2,1)} %v_hbm.1, bf16[256,4096]{1,0:T(8,128)(2,1)} %w_hbm.1), custom_call_target="tpu_custom_call" | custom-call | tf_op jit(solution)/shard_map/attention_layer/pallas_call | solution.py:481
  71.7 1.9 %copy.8 = bf16[512,512]{1,0:T(8,128)(2,1)} copy(bf16[512,512]{1,0:T(8,128)(2,1)} %attention_layer.1) | data formatting | bytes 1048576

commit v4 on v3

--- a/solution.py
+++ b/solution.py
@@ -134,10 +134,10 @@
             def _():
                 send_or_keep(*q_copy(i, m))
 
-    near_queries(True)
     for i in heads:
         for what in range(2):
             send_or_keep(*kv_copy(i, what))
+    near_queries(True)
     near_queries(False)
 
     def w_copy(n):
@@ -385,9 +385,6 @@
         event(i == 4, from_side, 6, 7)
         event(i == 5, lambda: arrived(q_buf.at[pl.ds(2 * ROWS, ROWS)], q_recv.at[2]))
 
-        event(i == 7, merge, 2)
-        event(i == 7, merge, 3)
-
         meet(
             [
                 keys_step(
@@ -408,6 +405,8 @@
             close(now((0, 0, 0, 0, 2, 6, 4, 5)))
             close(now((0, 0, 0, 0, 3, 7, 0, 1)))
 
+        event(i == 7, merge, 2)
+        event(i == 7, merge, 3)
         return carry
 
     lax.fori_loop(0, 8, step, 0)

time: 73.7 us -> 70.6 us (0.958)
  the two profiles are of different devices: /device:TPU:89 before, /device:TPU:1 now
where the time goes in v4:
time: 70.6 us; the launch traced here: 70.5 us
  Pallas kernels  68.6 us (97%)
  local copies, waits for them, and re-layouts  1.87 us (3%)
    pallas_call x1, Pallas kernels, per_device(): pl.pallas_call(kernel, out_shape=jax.ShapeDtypeStruct((ROWS, COLS), bf16)...  68.6 us
    unnamed x1, local copies, waits for them, and re-layouts  1.87 us

profile of v4, /device:TPU:1, one launch (start us, length us, event | category | flops | bytes accessed | tf_op | source)
XLA Modules:
  0.0 70.5 jit_solution(15520824674120497067)
XLA Ops:
  0.0 68.6 %attention_layer.1 = bf16[512,512]{1,0:T(8,128)(2,1)} custom-call(s32[64]{0:T(128)} %order_ref.1, s32[64]{0:T(128)} %frames_ref.1, bf16[512,256]{1,0:T(8,128)(2,1)} %q_hbm.1, bf16[512,256]{1,0:T(8,128)(2,1)} %k_hbm.1, bf16[512,256]{1,0:T(8,128)(2,1)} %v_hbm.1, bf16[256,4096]{1,0:T(8,128)(2,1)} %w_hbm.1), custom_call_target="tpu_custom_call" | custom-call | tf_op jit(solution)/shard_map/attention_layer/pallas_call | solution.py:480
  68.6 1.9 %copy.8 = bf16[512,512]{1,0:T(8,128)(2,1)} copy(bf16[512,512]{1,0:T(8,128)(2,1)} %attention_layer.1) | data formatting | bytes 1048576
